TPU v7x, 32 devices: a whole 2x2x4 slice. The times are simulated.
32 devices in a mesh: groups: 2 (over y), dp: 4 (over z), space: 2 (over x), pair: 2 (over core).
Axes of the slice: x: 2, y: 2, z: 4, core: 2. Of those that a mesh axis runs over, the one named last changes fastest.
Arguments:
- volume: bfloat16 [32, 8, 16, 16, 128], P(('groups', 'dp', 'pair'), 'space'), parts along dimension 0, may hold values from -6 to 6
- tissue: int32 [32, 2048], P(('groups', 'dp', 'pair'), 'space'), parts along dimension 0, may hold values 0 or 1
- brick_count: int32 [16], P(('groups', 'dp', 'pair')), parts along dimension 0, may hold values from 1 to 2, as said below
- first_weight: bfloat16 [3, 3, 3, 128, 128], replicated, may hold values from -0.109375 to 0.109375
- second_weight: bfloat16 [3, 3, 3, 128, 128], replicated, may hold values from -0.109375 to 0.109375
- cotangent: bfloat16 [32, 8, 16, 16, 128], P(('groups', 'dp', 'pair'), 'space'), parts along dimension 0, may hold values from -6 to 6
Outputs:
- input_grad: bfloat16 [32, 8, 16, 16, 128], P(('groups', 'dp', 'pair'), 'space'), parts along dimension 0
- first_weight_grad: float32 [6912, 128], P('groups'), parts along dimension 0
- second_weight_grad: float32 [6912, 128], P('groups'), parts along dimension 0
There are 2 independent parts, one for each index of `groups`. A program takes and returns all parts, laid end to end along the dimension named above; an argument that names none is the same for every part. Nothing has to cross between parts.
Inputs may be any that keep to these rules, and one draw needn't show every extreme that they name: `brick_count`: the number of active bricks of an owner; they are its first slots, the other slots are unused.
All inputs are finite; a program needn't handle non-finite values. No bound on the sum of `tissue` on one device may be relied on, other than what follows from the above.
Results may differ from a plain program's by a relative error of at most 0.0059.
Values may be sent and summed in bfloat16 or wider, within the bound.
A program may use at most 64 MiB of HBM per device.

v0:
```python
import jax
import jax.numpy as jnp
from jax import lax
from jax.sharding import PartitionSpec as P


def extended(block, sides, width):
    for axis, dim in sides:
        count = lax.axis_size(axis)
        forward = [(i, i + 1) for i in range(count - 1)]
        backward = [(target, source) for source, target in forward]
        low = lax.ppermute(
            lax.slice_in_dim(block, block.shape[dim] - width, None, axis=dim), axis, forward
        )
        high = lax.ppermute(lax.slice_in_dim(block, 0, width, axis=dim), axis, backward)
        block = jnp.concatenate([low, block, high], axis=dim)
    return block


def unfold_slab(padded_block, slab_depth, edge_cells):
    framed = jnp.pad(padded_block, ((0, 0), (1, 1), (1, 1), (0, 0)))
    pieces = []
    for shift_z in range(3):
        for shift_y in range(3):
            for shift_x in range(3):
                pieces.append(
                    framed[
                        shift_z : shift_z + slab_depth,
                        shift_y : shift_y + edge_cells,
                        shift_x : shift_x + edge_cells,
                        :,
                    ]
                )
    joined = jnp.concatenate(pieces, axis=-1)
    return joined.reshape(slab_depth * edge_cells * edge_cells, joined.shape[-1])


def slope(pre_act):
    sigmoid_of = jax.nn.sigmoid(pre_act)
    return sigmoid_of * (1.0 + pre_act * (1.0 - sigmoid_of))


def with_rims(buffer_now):
    return extended(buffer_now, (("space", 1),), 1)


def process(work_vol, work_cot, work_gate, flags, first_weight, second_weight, framing):
    entries, slab_depth, edge_cells, _, channels = work_vol.shape
    shape_one = (slab_depth, edge_cells, edge_cells, channels)
    cells = slab_depth * edge_cells * edge_cells
    work_order = jnp.argsort(1 - flags, stable=True)
    live_count = jnp.sum(flags)
    first_flat = first_weight.reshape(27 * channels, channels)
    second_flat = second_weight.reshape(27 * channels, channels)
    first_back = jnp.swapaxes(jnp.flip(first_weight, (0, 1, 2)), 3, 4).reshape(
        27 * channels, channels
    )
    second_back = jnp.swapaxes(jnp.flip(second_weight, (0, 1, 2)), 3, 4).reshape(
        27 * channels, channels
    )
    gating_all = work_gate.reshape(entries, slab_depth, edge_cells, edge_cells, 1).astype(
        jnp.float32
    )
    contract = (((0,), (0,)), ((), ()))
    zero_grad = jnp.zeros((27 * channels, channels), jnp.float32)
    vol_rims = framing(work_vol)

    def first_pass(turn_index, state_now):
        hidden_buf, pre_buf = state_now
        brick_id = work_order[turn_index]
        columns = unfold_slab(vol_rims[brick_id], slab_depth, edge_cells)
        pre_one = jnp.dot(columns, first_flat, preferred_element_type=jnp.float32).reshape(
            shape_one
        )
        hidden = (jax.nn.silu(pre_one) * gating_all[brick_id]).astype(jnp.bfloat16)
        return (hidden_buf.at[brick_id].set(hidden), pre_buf.at[brick_id].set(pre_one))

    hidden_buf, pre_buf = lax.fori_loop(
        0,
        live_count,
        first_pass,
        (jnp.zeros(work_vol.shape, jnp.bfloat16), jnp.zeros(work_vol.shape, jnp.float32)),
    )
    hidden_rims = framing(hidden_buf)

    def second_pass(turn_index, state_now):
        error_buf, grad_second = state_now
        brick_id = work_order[turn_index]
        hidden_cols = unfold_slab(hidden_rims[brick_id], slab_depth, edge_cells)
        pre_two = jnp.dot(hidden_cols, second_flat, preferred_element_type=jnp.float32).reshape(
            shape_one
        )
        error_two = (
            work_cot[brick_id].astype(jnp.float32) * gating_all[brick_id] * slope(pre_two)
        ).astype(jnp.bfloat16)
        grad_second = grad_second + lax.dot_general(
            hidden_cols,
            error_two.reshape(cells, channels),
            contract,
            preferred_element_type=jnp.float32,
        )
        return (error_buf.at[brick_id].set(error_two), grad_second)

    error_buf, grad_second = lax.fori_loop(
        0, live_count, second_pass, (jnp.zeros(work_vol.shape, jnp.bfloat16), zero_grad)
    )
    error_rims = framing(error_buf)

    def third_pass(turn_index, state_now):
        signal_buf, grad_first = state_now
        brick_id = work_order[turn_index]
        back_one = jnp.dot(
            unfold_slab(error_rims[brick_id], slab_depth, edge_cells),
            second_back,
            preferred_element_type=jnp.float32,
        ).reshape(shape_one)
        error_one = (back_one * gating_all[brick_id] * slope(pre_buf[brick_id])).astype(
            jnp.bfloat16
        )
        columns = unfold_slab(vol_rims[brick_id], slab_depth, edge_cells)
        grad_first = grad_first + lax.dot_general(
            columns,
            error_one.reshape(cells, channels),
            contract,
            preferred_element_type=jnp.float32,
        )
        return (signal_buf.at[brick_id].set(error_one), grad_first)

    signal_buf, grad_first = lax.fori_loop(
        0, live_count, third_pass, (jnp.zeros(work_vol.shape, jnp.bfloat16), zero_grad)
    )
    grad_first, grad_second = lax.psum((grad_first, grad_second), ("dp", "space", "pair"))
    signal_rims = framing(signal_buf)

    def fourth_pass(turn_index, input_buf):
        brick_id = work_order[turn_index]
        input_back = jnp.dot(
            unfold_slab(signal_rims[brick_id], slab_depth, edge_cells),
            first_back,
            preferred_element_type=jnp.float32,
        ).reshape(shape_one)
        return input_buf.at[brick_id].set(input_back.astype(jnp.bfloat16))

    input_buf = lax.fori_loop(0, live_count, fourth_pass, jnp.zeros(work_vol.shape, jnp.bfloat16))
    return (input_buf, grad_first, grad_second)


def split_run(work_vol, work_cot, work_gate, flags, first_weight, second_weight):
    return process(work_vol, work_cot, work_gate, flags, first_weight, second_weight, with_rims)


def local(volume, tissue, brick_count, first_weight, second_weight, cotangent):
    slot_count, slab_depth, edge_cells, _, channels = volume.shape
    live_own = brick_count[0]
    own_flags = (jnp.arange(slot_count, dtype=jnp.int32) < live_own).astype(jnp.int32)
    input_grad, grad_first, grad_second = split_run(
        volume, cotangent, tissue, own_flags, first_weight, second_weight
    )
    scale_factor = (slot_count * slab_depth * edge_cells * edge_cells) ** (-0.5)
    return (input_grad, grad_first * scale_factor, grad_second * scale_factor)


def solution(mesh):
    in_specs = (
        P(("groups", "dp", "pair"), "space", None, None, None),
        P(("groups", "dp", "pair"), "space"),
        P(("groups", "dp", "pair")),
        P(),
        P(),
        P(("groups", "dp", "pair"), "space", None, None, None),
    )
    out_specs = (
        P(("groups", "dp", "pair"), "space", None, None, None),
        P("groups", None),
        P("groups", None),
    )
    return jax.shard_map(local, mesh=mesh, in_specs=in_specs, out_specs=out_specs, check_vma=False)
```

profile of v0, /device:TPU:0, one launch (start us, length us, event | category | flops | bytes accessed | tf_op | source)
XLA Modules:
  0.0 251.7 jit_solution(138225401323282991)
XLA Ops:
  8.2 4.8 %collective-permute-start = (bf16[2,1,16,16,128]{4,3,2,1,0:T(8,128)(2,1)S(1)}, bf16[2,1,16,16,128]{4,3,2,1,0:T(8,128)(2,1)S(1)}, u32[]{:S(2)}, u32[]{:S(2)}) collective-permute-start(bf16[2,1,16,16,128]{4,3,2,1,0:T(8,128)(2,1)S(1)} %get-tuple-element.611), channel_id=1, source_target_pairs={{0,2},{1,3},{4,6},{5,7},{8,10},{9,11},{12,14},{13,15},{16,18},{17,... | collective-permute-start | bytes 393224 | tf_op jit(solution)/shard_map/ppermute | solution.py:12
  18.2 1.8 collective-permute-done.1
  20.1 23.6 %while.59 = (s32[]{:T(128)}, bf16[2,4,16,16,128]{4,3,2,1,0:T(8,128)(2,1)S(1)}, f32[2,4,16,16,128]{4,3,2,1,0:T(8,128)S(1)}, s32[]{:T(128)}, s32[2]{0:T(128)S(1)},...) while((s32[]{:T(128)}, ...), condition=%wide.region_4.5_spmd, body=%wide.region_2.4_spmd.sunk | while | flops 907018240 | bytes 38281604 | solution.py:78
  28.0 2.0 fusion.281
  39.5 2.0 fusion.281
  43.8 2.8 %collective-permute-start.2 = (bf16[2,1,16,16,128]{4,3,2,1,0:T(8,128)(2,1)S(1)}, bf16[2,1,16,16,128]{4,3,2,1,0:T(8,128)(2,1)S(1)}, u32[]{:S(2)}, u32[]{:S(2)}) collective-permute-start(bf16[2,1,16,16,128]{4,3,2,1,0:T(8,128)(2,1)S(1)} %get-tuple-element.608), channel_id=1, source_target_pairs={{0,2},{1,3},{4,6},{5,7},{8,10},{9,11},{12,14},{13,15},{16,18},{17,... | collective-permute-start | bytes 393224 | tf_op jit(solution)/shard_map/ppermute | solution.py:12
  49.1 4.4 %collective-permute-done.3 = bf16[2,1,16,16,128]{4,3,2,1,0:T(8,128)(2,1)S(1)} collective-permute-done((bf16[2,1,16,16,128]{4,3,2,1,0:T(8,128)(2,1)S(1)}, bf16[2,1,16,16,128]{4,3,2,1,0:T(8,128)(2,1)S(1)}, u32[]{:S(2)}, u32[]{:S(2)}) %collective-permute-start.3) | collective-permute-done | bytes 131104 | tf_op jit(solution)/shard_map/ppermute | solution.py:15
  53.6 1.3 broadcast_in_dim.6.clone
  55.0 28.6 %while.60 = (s32[]{:T(128)}, bf16[2,4,16,16,128]{4,3,2,1,0:T(8,128)(2,1)S(1)}, f32[3456,128]{1,0:T(8,128)}, s32[]{:T(128)}, s32[2]{0:T(128)S(1)}, /*index=5*/bf1...) while((s32[]{:T(128)}, ...), condition=%wide.region_7.8_spmd, body=%wide.region_5.7_spmd.sunk | while | flops 1815396352 | bytes 58630632 | solution.py:104
  58.3 1.3 and_reduce_fusion.9
  62.4 3.0 %fusion.313 = (bf16[2,4,16,16,128]{4,3,2,1,0:T(8,128)(2,1)S(1)}, f32[4,16,16,128]{3,2,1,0:T(8,128)S(1)}) fusion(bf16[2,4,16,16,128]{4,3,2,1,0:T(8,128)(2,1)S(1)} %get-tuple-element.948, s32[]{:T(128)} %select_n.78, f32[4,16,16]{2,1,0:T(8,128)S(1)} %dynamic-slice_bitcast_fusion.29, pred[]{:T(512)} %and_reduce_fusion.9, ...), kind=kOutput, calls=%fused_computation.95.clone.1 | convolution fusion | flops 907542528 | bytes 9306117 | tf_op jit(solution)/shard_map/while/body/dot_general | solution.py:90
  65.4 2.5 fusion.314
  72.2 1.3 and_reduce_fusion.9
  76.3 3.0 %fusion.313 = (bf16[2,4,16,16,128]{4,3,2,1,0:T(8,128)(2,1)S(1)}, f32[4,16,16,128]{3,2,1,0:T(8,128)S(1)}) fusion(bf16[2,4,16,16,128]{4,3,2,1,0:T(8,128)(2,1)S(1)} %get-tuple-element.948, s32[]{:T(128)} %select_n.78, f32[4,16,16]{2,1,0:T(8,128)S(1)} %dynamic-slice_bitcast_fusion.29, pred[]{:T(512)} %and_reduce_fusion.9, ...), kind=kOutput, calls=%fused_computation.95.clone.1 | convolution fusion | flops 907542528 | bytes 9306117 | tf_op jit(solution)/shard_map/while/body/dot_general | solution.py:90
  79.3 2.5 fusion.314
  83.6 1.5 collective-permute-start.4
  87.6 1.7 copy.9
  89.3 2.9 %collective-permute-done.5 = bf16[2,1,16,16,128]{4,3,2,1,0:T(8,128)(2,1)S(1)} collective-permute-done((bf16[2,1,16,16,128]{4,3,2,1,0:T(8,128)(2,1)S(1)}, bf16[2,1,16,16,128]{4,3,2,1,0:T(8,128)(2,1)S(1)}, u32[]{:S(2)}, u32[]{:S(2)}) %collective-permute-start.5) | collective-permute-done | bytes 131104 | tf_op jit(solution)/shard_map/ppermute | solution.py:15
  93.4 1.3 broadcast_in_dim.6
  94.7 32.4 %while.61 = (s32[]{:T(128)}, bf16[2,4,16,16,128]{4,3,2,1,0:T(8,128)(2,1)S(1)}, f32[3456,128]{1,0:T(8,128)}, s32[]{:T(128)}, s32[2]{0:T(128)S(1)}, /*index=5*/bf1...) while((s32[]{:T(128)}, ...), condition=%wide.region_10.11_spmd, body=%wide.region_8.10_spmd.sunk | while | flops 1813823488 | bytes 74064360 | solution.py:129
  101.6 2.9 %fusion.345 = (bf16[2,4,16,16,128]{4,3,2,1,0:T(8,128)(2,1)S(1)}, bf16[4,16,16,128]{3,2,1,0:T(8,128)(2,1)S(1)}) fusion(bf16[2,4,16,16,128]{4,3,2,1,0:T(8,128)(2,1)S(1)} %get-tuple-element.997, s32[]{:T(128)} %select_n.80, pred[]{:T(512)} %and_reduce_fusion.10, f32[2,4,16,16,128]{4,3,2,1,0:T(8,128)S(1)} %get-tuple-element.1021, ...), kind=kOutput, calls=%fused_computation.258.clone.1 | convolution fusion | flops 907411456 | bytes 9306117 | tf_op jit(solution)/shard_map/while/body/dot_general | solution.py:112
  107.2 2.3 fusion.373
  117.5 2.9 %fusion.345 = (bf16[2,4,16,16,128]{4,3,2,1,0:T(8,128)(2,1)S(1)}, bf16[4,16,16,128]{3,2,1,0:T(8,128)(2,1)S(1)}) fusion(bf16[2,4,16,16,128]{4,3,2,1,0:T(8,128)(2,1)S(1)} %get-tuple-element.997, s32[]{:T(128)} %select_n.80, pred[]{:T(512)} %and_reduce_fusion.10, f32[2,4,16,16,128]{4,3,2,1,0:T(8,128)S(1)} %get-tuple-element.1021, ...), kind=kOutput, calls=%fused_computation.258.clone.1 | convolution fusion | flops 907411456 | bytes 9306117 | tf_op jit(solution)/shard_map/while/body/dot_general | solution.py:112
  123.1 2.3 fusion.373
  127.1 1.7 collective-permute-start.6
  131.4 1.4 copy.10
  132.8 2.9 %collective-permute-done.7 = bf16[2,1,16,16,128]{4,3,2,1,0:T(8,128)(2,1)S(1)} collective-permute-done((bf16[2,1,16,16,128]{4,3,2,1,0:T(8,128)(2,1)S(1)}, bf16[2,1,16,16,128]{4,3,2,1,0:T(8,128)(2,1)S(1)}, u32[]{:S(2)}, u32[]{:S(2)}) %collective-permute-start.7) | collective-permute-done | bytes 131104 | tf_op jit(solution)/shard_map/ppermute | solution.py:15
  135.9 19.3 %while.62 = (s32[]{:T(128)}, bf16[2,4,16,16,128]{4,3,2,1,0:T(8,128)(2,1)S(1)}, s32[]{:T(128)}, s32[2]{0:T(128)S(1)}, bf16[2,6,16,16,128]{4,3,2,1,0:T(8,128)(2,1)...) while((s32[]{:T(128)}, ...), condition=%wide.region_13.14_spmd, body=%wide.region_11.13_spmd.sunk | while | flops 906231808 | bytes 26575192 | solution.py:144
  142.7 2.7 %fusion.403 = bf16[2,4,16,16,128]{4,3,2,1,0:T(8,128)(2,1)S(1)} fusion(bf16[2,4,16,16,128]{4,3,2,1,0:T(8,128)(2,1)S(1)} %get-tuple-element.1044, s32[]{:T(128)} %select_n.82, bf16[4,16,16,3456]{3,2,1,0:T(8,128)(2,1)S(1)} %fusion.402, bf16[3456,128]{1,0:T(8,128)(2,1)S(1)} %get-tuple-element.1061, pred[]{:T(512)} %and_reduce_fusion.11), kind=kOutput, calls=%fused_computation.288.clone.1 | convolution fusion | flops 906231808 | bytes 8486917 | tf_op jit(solution)/shard_map/while/body/dot_general | solution.py:137
  152.0 2.7 %fusion.403 = bf16[2,4,16,16,128]{4,3,2,1,0:T(8,128)(2,1)S(1)} fusion(bf16[2,4,16,16,128]{4,3,2,1,0:T(8,128)(2,1)S(1)} %get-tuple-element.1044, s32[]{:T(128)} %select_n.82, bf16[4,16,16,3456]{3,2,1,0:T(8,128)(2,1)S(1)} %fusion.402, bf16[3456,128]{1,0:T(8,128)(2,1)S(1)} %get-tuple-element.1061, pred[]{:T(512)} %and_reduce_fusion.11), kind=kOutput, calls=%fused_computation.288.clone.1 | convolution fusion | flops 906231808 | bytes 8486917 | tf_op jit(solution)/shard_map/while/body/dot_general | solution.py:137
  155.2 85.6 %all-reduce.8.cloned.1.call-done = (f32[3456,128]{1,0:T(8,128)}, f32[3456,128]{1,0:T(8,128)}) async-done(((f32[3456,128]{1,0:T(8,128)}, f32[3456,128]{1,0:T(8,128)}), (f32[3456,128]{1,0:T(8,128)}, f32[3456,128]{1,0:T(8,128)})) %all-reduce.8.cloned.1.call-update) | async-done | bytes 3538960 | tf_op jit(solution)/shard_map/psum | solution.py:132
  240.8 4.1 %broadcast_multiply_fusion = (f32[3456,128]{1,0:T(8,128)}, f32[3456,128]{1,0:T(8,128)}) fusion(f32[3456,128]{1,0:T(8,128)} %get-tuple-element.570, f32[3456,128]{1,0:T(8,128)} %get-tuple-element.569), kind=kLoop, calls=%fused_computation.322 | loop fusion | flops 884736 | bytes 7077888 | tf_op jit(solution)/shard_map/mul | solution.py:160
  (387 shorter events, 60.8 us)
Async XLA Ops:
  7.2 233.6 %all-reduce.8.cloned.1.call-start = ((), (), s32[]{:S(2)}) async-start(), calls=%async_computation | async-start | bytes 7077888 | tf_op jit(solution)/shard_map/psum | solution.py:132
  8.2 8.8 %collective-permute-start = (bf16[2,1,16,16,128]{4,3,2,1,0:T(8,128)(2,1)S(1)}, bf16[2,1,16,16,128]{4,3,2,1,0:T(8,128)(2,1)S(1)}, u32[]{:S(2)}, u32[]{:S(2)}) collective-permute-start(bf16[2,1,16,16,128]{4,3,2,1,0:T(8,128)(2,1)S(1)} %get-tuple-element.611), channel_id=1, source_target_pairs={{0,2},{1,3},{4,6},{5,7},{8,10},{9,11},{12,14},{13,15},{16,18},{17,... | collective-permute-start | bytes 393224 | tf_op jit(solution)/shard_map/ppermute | solution.py:12
  13.1 6.9 %collective-permute-start.1 = (bf16[2,1,16,16,128]{4,3,2,1,0:T(8,128)(2,1)S(1)}, bf16[2,1,16,16,128]{4,3,2,1,0:T(8,128)(2,1)S(1)}, u32[]{:S(2)}, u32[]{:S(2)}) collective-permute-start(bf16[2,1,16,16,128]{4,3,2,1,0:T(8,128)(2,1)S(1)} %get-tuple-element.610), channel_id=1, source_target_pairs={{2,0},{3,1},{6,4},{7,5},{10,8},{11,9},{14,12},{15,13},{18,16},{19,... | collective-permute-start | bytes 393224 | tf_op jit(solution)/shard_map/ppermute | solution.py:15
  26.0 1.9 copy-start.6
  37.5 1.9 copy-start.6
  43.8 5.3 %collective-permute-start.2 = (bf16[2,1,16,16,128]{4,3,2,1,0:T(8,128)(2,1)S(1)}, bf16[2,1,16,16,128]{4,3,2,1,0:T(8,128)(2,1)S(1)}, u32[]{:S(2)}, u32[]{:S(2)}) collective-permute-start(bf16[2,1,16,16,128]{4,3,2,1,0:T(8,128)(2,1)S(1)} %get-tuple-element.608), channel_id=1, source_target_pairs={{0,2},{1,3},{4,6},{5,7},{8,10},{9,11},{12,14},{13,15},{16,18},{17,... | collective-permute-start | bytes 393224 | tf_op jit(solution)/shard_map/ppermute | solution.py:12
  46.6 6.9 %collective-permute-start.3 = (bf16[2,1,16,16,128]{4,3,2,1,0:T(8,128)(2,1)S(1)}, bf16[2,1,16,16,128]{4,3,2,1,0:T(8,128)(2,1)S(1)}, u32[]{:S(2)}, u32[]{:S(2)}) collective-permute-start(bf16[2,1,16,16,128]{4,3,2,1,0:T(8,128)(2,1)S(1)} %get-tuple-element.609), channel_id=1, source_target_pairs={{2,0},{3,1},{6,4},{7,5},{10,8},{11,9},{14,12},{15,13},{18,16},{19,... | collective-permute-start | bytes 393224 | tf_op jit(solution)/shard_map/ppermute | solution.py:15
  60.1 2.3 copy-start.5
  60.1 2.3 copy-start.9
  62.1 3.3 %copy-start.2 = (f32[3456,128]{1,0:T(8,128)S(1)}, f32[3456,128]{1,0:T(8,128)}, u32[]{:S(2)}) copy-start(f32[3456,128]{1,0:T(8,128)} %get-tuple-element.949) | copy-start | bytes 5308420 | tf_op jit(solution)/shard_map/while
  67.9 1.2 copy-start.3
  74.0 2.3 copy-start.5
  74.1 2.3 copy-start.9
  76.0 3.3 %copy-start.2 = (f32[3456,128]{1,0:T(8,128)S(1)}, f32[3456,128]{1,0:T(8,128)}, u32[]{:S(2)}) copy-start(f32[3456,128]{1,0:T(8,128)} %get-tuple-element.949) | copy-start | bytes 5308420 | tf_op jit(solution)/shard_map/while
  81.8 1.2 copy-start.3
  83.5 1.6 copy-start.4
  83.6 11.1 %copy-start.10 = (s32[5]{0:T(128)S(1)}, s32[5]{0:T(128)}, u32[]{:S(2)}) copy-start(s32[5]{0:T(128)} %get-tuple-element.1101) | copy-start | bytes 64
  83.6 5.7 %collective-permute-start.4 = (bf16[2,1,16,16,128]{4,3,2,1,0:T(8,128)(2,1)S(1)}, bf16[2,1,16,16,128]{4,3,2,1,0:T(8,128)(2,1)S(1)}, u32[]{:S(2)}, u32[]{:S(2)}) collective-permute-start(bf16[2,1,16,16,128]{4,3,2,1,0:T(8,128)(2,1)S(1)} %get-tuple-element.606), channel_id=1, source_target_pairs={{0,2},{1,3},{4,6},{5,7},{8,10},{9,11},{12,14},{13,15},{16,18},{17,... | collective-permute-start | bytes 393224 | tf_op jit(solution)/shard_map/ppermute | solution.py:12
  85.1 7.0 %collective-permute-start.5 = (bf16[2,1,16,16,128]{4,3,2,1,0:T(8,128)(2,1)S(1)}, bf16[2,1,16,16,128]{4,3,2,1,0:T(8,128)(2,1)S(1)}, u32[]{:S(2)}, u32[]{:S(2)}) collective-permute-start(bf16[2,1,16,16,128]{4,3,2,1,0:T(8,128)(2,1)S(1)} %get-tuple-element.607), channel_id=1, source_target_pairs={{2,0},{3,1},{6,4},{7,5},{10,8},{11,9},{14,12},{15,13},{18,16},{19,... | collective-permute-start | bytes 393224 | tf_op jit(solution)/shard_map/ppermute | solution.py:15
  99.4 2.2 copy-start.7
  105.0 2.3 copy-start
  109.5 1.2 copy-start.1
  115.2 2.2 copy-start.7
  120.8 2.3 copy-start
  125.3 1.2 copy-start.1
  127.1 5.7 %collective-permute-start.6 = (bf16[2,1,16,16,128]{4,3,2,1,0:T(8,128)(2,1)S(1)}, bf16[2,1,16,16,128]{4,3,2,1,0:T(8,128)(2,1)S(1)}, u32[]{:S(2)}, u32[]{:S(2)}) collective-permute-start(bf16[2,1,16,16,128]{4,3,2,1,0:T(8,128)(2,1)S(1)} %get-tuple-element.604), channel_id=1, source_target_pairs={{0,2},{1,3},{4,6},{5,7},{8,10},{9,11},{12,14},{13,15},{16,18},{17,... | collective-permute-start | bytes 393224 | tf_op jit(solution)/shard_map/ppermute | solution.py:12
  128.8 6.9 %collective-permute-start.7 = (bf16[2,1,16,16,128]{4,3,2,1,0:T(8,128)(2,1)S(1)}, bf16[2,1,16,16,128]{4,3,2,1,0:T(8,128)(2,1)S(1)}, u32[]{:S(2)}, u32[]{:S(2)}) collective-permute-start(bf16[2,1,16,16,128]{4,3,2,1,0:T(8,128)(2,1)S(1)} %get-tuple-element.605), channel_id=1, source_target_pairs={{2,0},{3,1},{6,4},{7,5},{10,8},{11,9},{14,12},{15,13},{18,16},{19,... | collective-permute-start | bytes 393224 | tf_op jit(solution)/shard_map/ppermute | solution.py:15
  155.2 89.7 %copy-start.8 = (bf16[2,4,16,16,128]{4,3,2,1,0:T(8,128)(2,1)}, bf16[2,4,16,16,128]{4,3,2,1,0:T(8,128)(2,1)S(1)}, u32[]{:S(2)}) copy-start(bf16[2,4,16,16,128]{4,3,2,1,0:T(8,128)(2,1)S(1)} %get-tuple-element.492) | copy-start | bytes 1572868
Sparse Core Ops, SparseCore 0:
  132.9 107.7 all-reduce.7
where the time goes:
time: 253 us; the launch traced here: 252 us
  waiting for transfers between devices  98.7 us (39%)
  local copies, waits for them, and re-layouts  48 us (19%)
  matrix products  30.4 us (12%)
  loops' own time  24.9 us (10%)
  other arithmetic  18.7 us (7%)
  starting transfers between devices  16.1 us (6%)
  between operations  14.9 us (6%)
    psum x1, waiting for transfers between devices, process(): lax.psum((grad_first, grad_second), ('dp', 'space', 'pair'))  85.6 us
    while x292, local copies, waits for them, and re-layouts  27.6 us
    ppermute x4, waiting for transfers between devices, extended(): lax.ppermute(lax.slice_in_dim(block, 0, width, axis=dim), axis, backward)  11.9 us
    ppermute x4, starting transfers between devices, extended(): lax.ppermute(lax.slice_in_dim(block, block.shape[dim] - width, None, axis...  10.8 us
    another operation x8, other arithmetic  7.99 us
    another operation x1, loops' own time, process(): lax.fori_loop(0, live_count, third_pass, (jnp.zeros(work_vol.shape, jnp.b...  6.48 us
    another operation x1, loops' own time, process(): lax.fori_loop(0, live_count, second_pass, (jnp.zeros(work_vol.shape, jnp....  6.22 us
    another operation x1, loops' own time, process(): lax.fori_loop(0, live_count, fourth_pass, jnp.zeros(work_vol.shape, jnp.b...  6.14 us
  transfers between devices with their start and end apart: 9, of which 6 were waited for; matrix products, arithmetic and copies ran while one was open for 9% of the time, Pallas kernels for 0%

commit v1 on v0

v1 whole, which is shorter than its diff:
```python
import functools

import jax
import jax.numpy as jnp
from jax import lax
from jax.experimental import pallas as pl
from jax.experimental.pallas import tpu as pltpu
from jax.sharding import PartitionSpec as P

BF = jnp.bfloat16
F32 = jnp.float32
MESH = pl.DeviceIdType.MESH


def remote(src, dst, send_sem, recv_sem, where):
    return pltpu.make_async_remote_copy(
        src_ref=src, dst_ref=dst, send_sem=send_sem, recv_sem=recv_sem,
        device_id=where, device_id_type=MESH,
    )


def kernel(D, S, N2, vol, cot, gate, w1, w2, out, g1, g2,
           fv, fh, fe2, fe1, k1, k2, k2b, k1b, sg1, e1t, e2t, grad,
           edges, halo, ps, pr, xs, xr, zs, zr,
           hs_sem, hr_sem, p_s, p_r, x_s, x_r, z_s, z_r, za_s, za_r, xa_s, xa_r, pa_s, pa_r):
    B, Z, M, C = vol.shape
    E = fv.shape[3]
    d, x, c = lax.axis_index("dp"), lax.axis_index("space"), lax.axis_index("pair")
    RC = N2
    R2 = RC // S
    R3 = R2 // D

    barrier = pltpu.get_barrier_semaphore()
    pl.semaphore_signal(barrier, inc=1, device_id={"pair": 1 - c}, device_id_type=MESH)
    for k in range(1, S):
        pl.semaphore_signal(barrier, inc=1, device_id={"space": lax.rem(x + k, S)}, device_id_type=MESH)
    for k in range(1, D):
        pl.semaphore_signal(barrier, inc=1, device_id={"dp": lax.rem(d + k, D)}, device_id_type=MESH)
    pl.semaphore_wait(barrier, 1 + (S - 1) + (D - 1))

    def halo_copies(f, b):
        if f == 0:
            top, bottom = vol.at[b, Z - 1], vol.at[b, 0]
        else:
            top, bottom = edges.at[f - 1, b, 1], edges.at[f - 1, b, 0]
        up = remote(top, halo.at[f, b, 0], hs_sem.at[f, b, 0], hr_sem.at[f, b, 0],
                    {"space": jnp.minimum(x + 1, S - 1)})
        down = remote(bottom, halo.at[f, b, 1], hs_sem.at[f, b, 1], hr_sem.at[f, b, 1],
                      {"space": jnp.maximum(x - 1, 0)})
        return up, down

    def halo_start(f, b):
        up, down = halo_copies(f, b)

        @pl.when(x < S - 1)
        def _():
            up.start()

        @pl.when(x > 0)
        def _():
            down.start()

    row = lax.rem(lax.broadcasted_iota(jnp.int32, (M, C), 0), E)

    def put(field, b, z, val):
        low = jnp.where(row == 0, 0.0, pltpu.roll(val, 1, 0)).astype(BF)
        high = jnp.where(row == E - 1, 0.0, pltpu.roll(val, M - 1, 0)).astype(BF)
        field[b, z, 1 : E + 1] = jnp.concatenate([low, val.astype(BF), high], axis=-1).reshape(E, E, 3 * C)

    def halo_finish(f, field, b):
        up, down = halo_copies(f, b)

        @pl.when(x < S - 1)
        def _():
            up.wait_send()
            down.wait_recv()
            put(field, b, Z + 1, halo[f, b, 1].astype(F32))

        @pl.when(x > 0)
        def _():
            down.wait_send()
            up.wait_recv()
            put(field, b, 0, halo[f, b, 0].astype(F32))

    for b in range(B):
        halo_start(0, b)

    for field in (fv, fh, fe2, fe1):
        for b in range(B):
            zero_row = jnp.zeros((Z + 2, E, 3 * C), BF)
            field[b, :, 0] = zero_row
            field[b, :, E + 1] = zero_row

            @pl.when(x == 0)
            def _():
                field[b, 0] = jnp.zeros((E + 2, E, 3 * C), BF)

            @pl.when(x == S - 1)
            def _():
                field[b, Z + 1] = jnp.zeros((E + 2, E, 3 * C), BF)

    for wide in (k1, k2, k2b, k1b):
        wide[27 * C :, :C] = jnp.zeros((9 * C, C), BF)
        wide[: 9 * C, C:] = jnp.zeros((9 * C, C), BF)

    def build(o, carry):
        at = pl.ds(pl.multiple_of(o * C, C), C)
        later = pl.ds(pl.multiple_of((o + 9) * C, C), C)
        back = pl.ds(pl.multiple_of((26 - o) * C, C), C)
        back_later = pl.ds(pl.multiple_of((35 - o) * C, C), C)
        for src, wide, wide_back in ((w1, k1, k1b), (w2, k2, k2b)):
            block = src[at, :]
            wide[at, :C] = block
            wide[later, C:] = block
            turned = block.T
            wide_back[back, :C] = turned
            wide_back[back_later, C:] = turned
        return carry

    lax.fori_loop(0, 27, build, 0)

    def fill(i, carry):
        b, z = i // Z, lax.rem(i, Z)
        put(fv, b, z + 1, vol[b, z].astype(F32))
        return carry

    lax.fori_loop(0, B * Z, fill, 0)

    def conv(field, b, zp, wide):
        parts = []
        for l in range(4):
            for dy in range(3):
                parts.append(field[b, 2 * zp + l, dy : dy + E].reshape(M, 3 * C))
        got = jnp.dot(jnp.concatenate(parts, axis=-1), wide[...], preferred_element_type=F32)
        return got[:, :C], got[:, C:]

    def phase(f, b, field, wide, use):
        halo_finish(f, field, b)

        def body(zp, carry):
            for t, val in enumerate(conv(field, b, zp, wide)):
                use(b, 2 * zp + t, val)
            return carry

        lax.fori_loop(0, Z // 2, body, 0)

    def after(f, b, field):
        edges[f - 1, b, 0] = field[b, 1, 1 : E + 1].reshape(M, 3 * C)[:, C : 2 * C]
        edges[f - 1, b, 1] = field[b, Z, 1 : E + 1].reshape(M, 3 * C)[:, C : 2 * C]
        halo_start(f, b)

    def use_one(b, z, pre):
        s = jax.nn.sigmoid(pre)
        gating = gate[b, z].astype(F32)
        sg1[b, z] = gating * (s * (1.0 + pre * (1.0 - s)))
        put(fh, b, z + 1, pre * s * gating)

    def lanes(b, z):
        return pl.ds(pl.multiple_of((b * Z + z) * M, M), M)

    def use_two(b, z, pre):
        s = jax.nn.sigmoid(pre)
        val = cot[b, z].astype(F32) * gate[b, z].astype(F32) * (s * (1.0 + pre * (1.0 - s)))
        put(fe2, b, z + 1, val)
        e2t[:, lanes(b, z)] = val.T.astype(BF)

    def use_three(b, z, back):
        val = back * sg1[b, z]
        put(fe1, b, z + 1, val)
        e1t[:, lanes(b, z)] = val.T.astype(BF)

    def use_four(b, z, back):
        out[b, z] = back.astype(BF)

    def gradient(g, field, turned):
        def body(i, carry):
            dz, dy = i // 3, lax.rem(i, 3)
            total = None
            for b in range(B):
                cols = field[b, pl.ds(dz, Z), pl.ds(dy, E)].reshape(Z * M, 3 * C)
                term = jnp.dot(turned[:, b * Z * M : (b + 1) * Z * M], cols, preferred_element_type=F32)
                total = term if total is None else total + term
            for dx in range(3):
                grad[g, pl.ds(pl.multiple_of((i * 3 + dx) * C, C), C), :] = total[:, dx * C : (dx + 1) * C]
            return carry

        lax.fori_loop(0, 9, body, 0)

    outs = (g1, g2)

    def pair_copy(g):
        return remote(ps.at[g], pr.at[g], p_s.at[g], p_r.at[g], {"pair": 1 - c})

    def pair_start(g):
        ps[g] = grad[g, pl.ds(pl.multiple_of((1 - c) * RC, 16), RC), :].astype(BF)
        pair_copy(g).start()

    def space_copy(g, k):
        to = lax.rem(x + k, S)
        return remote(xs.at[g, to], xr.at[g, k - 1], x_s.at[g, k - 1], x_r.at[g, k - 1], {"space": to})

    def mine(g):
        return grad.at[g, pl.ds(pl.multiple_of(c * RC, 16), RC), :]

    def space_start(g):
        pair_copy(g).wait()
        total = mine(g)[...] + pr[g].astype(F32)
        mine(g)[...] = total
        xs[g] = total.astype(BF).reshape(S, R2, C)
        for k in range(1, S):
            space_copy(g, k).start()

    def dp_copy(g, k):
        to = lax.rem(d + k, D)
        return remote(zs.at[g, to], zr.at[g, k - 1], z_s.at[g, k - 1], z_r.at[g, k - 1], {"dp": to})

    def mid(g):
        return grad.at[g, pl.ds(pl.multiple_of(c * RC + x * R2, 16), R2), :]

    def dp_start(g):
        total = mid(g)[...]
        for k in range(1, S):
            space_copy(g, k).wait()
            total = total + xr[g, k - 1].astype(F32)
        mid(g)[...] = total
        zs[g] = total.astype(BF).reshape(D, R3, C)
        for k in range(1, D):
            dp_copy(g, k).start()

    def dp_gather(g, k, owner):
        spot = outs[g].at[c, x, owner]
        return remote(spot, spot, za_s.at[g, k - 1], za_r.at[g, k - 1], {"dp": lax.rem(d + k, D)})

    def gather_start(g):
        total = grad[g, pl.ds(pl.multiple_of(c * RC + x * R2 + d * R3, 16), R3), :]
        for k in range(1, D):
            dp_copy(g, k).wait()
            total = total + zr[g, k - 1].astype(F32)
        outs[g][c, x, d] = total.astype(BF)
        for k in range(1, D):
            dp_gather(g, k, d).start()

    def space_gather(g, k, owner):
        spot = outs[g].at[c, owner]
        return remote(spot, spot, xa_s.at[g, k - 1], xa_r.at[g, k - 1], {"space": lax.rem(x + k, S)})

    def space_gather_start(g):
        for k in range(1, D):
            dp_gather(g, k, d).wait_send()
            dp_gather(g, k, lax.rem(d - k + D, D)).wait_recv()
        for k in range(1, S):
            space_gather(g, k, x).start()

    def pair_gather(g, owner):
        spot = outs[g].at[owner]
        return remote(spot, spot, pa_s.at[g], pa_r.at[g], {"pair": 1 - c})

    def pair_gather_start(g):
        for k in range(1, S):
            space_gather(g, k, x).wait_send()
            space_gather(g, k, lax.rem(x - k + S, S)).wait_recv()
        pair_gather(g, c).start()

    def finish(g):
        pair_gather(g, c).wait_send()
        pair_gather(g, 1 - c).wait_recv()

    pad = 2 * RC - 27 * C
    if pad:
        for g in range(2):
            grad[g, 27 * C :, :] = jnp.zeros((pad, C), F32)

    for b in range(B):
        phase(0, b, fv, k1, use_one)
        after(1, b, fh)
    for b in range(B):
        phase(1, b, fh, k2, use_two)
        after(2, b, fe2)
    gradient(1, fh, e2t)
    pair_start(1)
    for b in range(B):
        phase(2, b, fe2, k2b, use_three)
        after(3, b, fe1)
        if b == 0:
            space_start(1)
    dp_start(1)
    gradient(0, fv, e1t)
    pair_start(0)
    gather_start(1)
    phase(3, 0, fe1, k1b, use_four)
    space_start(0)
    space_gather_start(1)
    for b in range(1, B):
        phase(3, b, fe1, k1b, use_four)
    dp_start(0)
    pair_gather_start(1)
    gather_start(0)
    space_gather_start(0)
    pair_gather_start(0)
    finish(1)
    finish(0)


def local(D, S, volume, tissue, brick_count, first_weight, second_weight, cotangent):
    B, Z, E, _, C = volume.shape
    M = E * E
    active = (jnp.arange(B, dtype=jnp.int32) < brick_count[0]).astype(jnp.int32)
    gate = jnp.broadcast_to((tissue * active[:, None]).astype(BF).reshape(B, Z, M, 1), (B, Z, M, C))
    unit = 16 * D * S
    RC = -(-27 * C // (2 * unit)) * unit
    R3 = RC // (D * S)
    field = pltpu.VMEM((B, Z + 2, E + 2, E, 3 * C), BF)
    wide = pltpu.VMEM((36 * C, 2 * C), BF)
    dma = pltpu.SemaphoreType.DMA
    s1, d1 = max(S - 1, 1), max(D - 1, 1)
    in_grad, g1, g2 = pl.pallas_call(
        functools.partial(kernel, D, S, RC),
        out_shape=(
            jax.ShapeDtypeStruct((B, Z, M, C), BF),
            jax.ShapeDtypeStruct((2, S, D, R3, C), BF),
            jax.ShapeDtypeStruct((2, S, D, R3, C), BF),
        ),
        in_specs=[pl.BlockSpec(memory_space=pltpu.VMEM)] * 5,
        out_specs=tuple([pl.BlockSpec(memory_space=pltpu.VMEM)] * 3),
        scratch_shapes=[
            field, field, field, field, wide, wide, wide, wide,
            pltpu.VMEM((B, Z, M, C), F32),
            pltpu.VMEM((C, B * Z * M), BF),
            pltpu.VMEM((C, B * Z * M), BF),
            pltpu.VMEM((2, 2 * RC, C), F32),
            pltpu.VMEM((3, B, 2, M, C), BF),
            pltpu.VMEM((4, B, 2, M, C), BF),
            pltpu.VMEM((2, RC, C), BF),
            pltpu.VMEM((2, RC, C), BF),
            pltpu.VMEM((2, S, RC // S, C), BF),
            pltpu.VMEM((2, s1, RC // S, C), BF),
            pltpu.VMEM((2, D, R3, C), BF),
            pltpu.VMEM((2, d1, R3, C), BF),
            dma((4, B, 2)), dma((4, B, 2)),
            dma((2,)), dma((2,)),
            dma((2, s1)), dma((2, s1)),
            dma((2, d1)), dma((2, d1)),
            dma((2, d1)), dma((2, d1)),
            dma((2, s1)), dma((2, s1)),
            dma((2,)), dma((2,)),
        ],
        compiler_params=pltpu.CompilerParams(
            collective_id=0, has_side_effects=True, vmem_limit_bytes=56 * 1024 * 1024
        ),
    )(
        volume.reshape(B, Z, M, C),
        cotangent.reshape(B, Z, M, C),
        gate,
        first_weight.reshape(27 * C, C),
        second_weight.reshape(27 * C, C),
    )
    scale = 2048 ** -0.5

    def finished(g):
        blocks = g.reshape(2 * RC, C)[: 27 * C].reshape(27, C, C)
        return (jnp.swapaxes(blocks, 1, 2).astype(F32) * scale).reshape(27 * C, C)

    return in_grad.reshape(volume.shape), finished(g1), finished(g2)


def solution(mesh):
    bricks = P(("groups", "dp", "pair"), "space", None, None, None)
    in_specs = (
        bricks,
        P(("groups", "dp", "pair"), "space"),
        P(("groups", "dp", "pair")),
        P(),
        P(),
        bricks,
    )
    out_specs = (bricks, P("groups", None), P("groups", None))
    run = functools.partial(local, mesh.shape["dp"], mesh.shape["space"])
    return jax.shard_map(run, mesh=mesh, in_specs=in_specs, out_specs=out_specs, check_vma=False)
```

time: 253 us -> 77.2 us (0.31)
  waiting for transfers between devices: 98.7 us -> 0 us
  Pallas kernels: 0 us -> 67.7 us
  local copies, waits for them, and re-layouts: 48 us -> 5.8 us
  matrix products: 30.4 us -> 0 us
  loops' own time: 24.9 us -> 0 us
  other arithmetic: 18.7 us -> 2.22 us
  starting transfers between devices: 16.1 us -> 0 us
  between operations: 14.9 us -> 1.32 us
    psum x1 -> x0, waiting for transfers between devices: 85.6 us -> none  [process(): lax.psum((grad_first, grad_second), ('dp', 'space', 'pair'))]
    pallas_call x0 -> x1, Pallas kernels: none -> 67.7 us  [local(): pl.pallas_call(functools.partial(kernel, D, S, RC), out_shape=(jax.ShapeD...]
    dot_general x12 -> x0, matrix products: 30.4 us -> none  [the longest x2 5.91 us: second_pass(): jnp.dot(hidden_cols, second_flat, preferred_element_type=jnp.float32)]
    while x292 -> x0, local copies, waits for them, and re-layouts: 27.6 us -> none
    another operation x4 -> x0, loops' own time: 24.9 us -> none  [the longest x1 6.48 us: process(): lax.fori_loop(0, live_count, third_pass, (jnp.zeros(work_vol.shape, jnp.b...]
    ppermute x8 -> x0, starting transfers between devices: 16 us -> none  [the longest x4 10.8 us: extended(): lax.ppermute(lax.slice_in_dim(block, block.shape[dim] - width, None, axis...]
    ppermute x8 -> x0, waiting for transfers between devices: 13.1 us -> none  [the longest x4 11.9 us: extended(): lax.ppermute(lax.slice_in_dim(block, 0, width, axis=dim), axis, backward)]
    another operation x8 -> x0, other arithmetic: 7.99 us -> none
  transfers between devices with their start and end apart: 9 -> 0, of which waited for: 6 -> 0; matrix products, arithmetic and copies ran while one was open for 9% -> 0% of each run, Pallas kernels for 0% -> 0%
where the time goes in v1:
time: 77.2 us; the launch traced here: 77 us
  Pallas kernels  67.7 us (88%)
  local copies, waits for them, and re-layouts  5.8 us (8%)
  other arithmetic  2.22 us (3%)
  between operations  1.32 us (2%)
    pallas_call x1, Pallas kernels, local(): pl.pallas_call(functools.partial(kernel, D, S, RC), out_shape=(jax.ShapeD...  67.7 us
    mul x2, local copies, waits for them, and re-layouts, finished(): return (jnp.swapaxes(blocks, 1, 2).astype(F32) * scale).reshape(27 * C, C)  3.85 us

profile of v1, /device:TPU:0, one launch (start us, length us, event | category | flops | bytes accessed | tf_op | source)
XLA Modules:
  0.0 77.0 jit_solution(15656267635185859192)
XLA Ops:
  1.3 0.8 %multiply_convert_fusion = bf16[2,1024]{1,0:T(2,128)(2,1)S(1)} fusion(s32[2,1024]{1,0:T(2,128)} %param.7, s32[2]{0:T(128)S(1)} %compare_convert_fusion), kind=kLoop, calls=%fused_computation.2 | loop fusion | flops 4096 | bytes 12296 | tf_op jit(solution)/shard_map/convert_element_type | solution.py:308
  2.1 1.1 %broadcast_in_dim.9.gate = bf16[2,4,256,128]{3,2,1,0:T(8,128)(2,1)} broadcast(bf16[2,4,256]{2,1,0:T(4,128)(2,1)S(1)} %broadcast_in_dim.8), dimensions={0,1,2} | broadcast | bytes 528384 | tf_op jit(solution)/shard_map/broadcast_in_dim | solution.py:308
  3.2 67.7 %shard_map.85 = (bf16[2,4,256,128]{3,2,1,0:T(8,128)(2,1)}, bf16[2,2,4,224,128]{4,3,2,1,0:T(8,128)(2,1)}, bf16[2,2,4,224,128]{4,3,2,1,0:T(8,128)(2,1)}) custom-call(bf16[2,4,256,128]{3,2,1,0:T(8,128)(2,1)} %bitcast.25, bf16[2,4,256,128]{3,2,1,0:T(8,128)(2,1)} %bitcast.26, bf16[2,4,256,128]{3,2,1,0:T(8,128)(2,1)} %broadcast_in_dim.9.gate, ...), custom_call_target="tpu_custom_call" | custom-call | tf_op jit(solution)/shard_map/pallas_call | solution.py:316
  70.9 1.3 %convert_multiply_fusion.1 = f32[3456,128]{1,0:T(8,128)S(1)} fusion(bf16[3584,128]{1,0:T(8,128)(2,1)} %bitcast.24), kind=kLoop, calls=%fused_computation.1 | loop fusion | flops 884736 | bytes 2654208 | tf_op jit(solution)/shard_map/mul | solution.py:361
  72.2 0.0 copy-start
  72.2 1.9 %copy.9 = f32[27,128,128]{1,2,0:T(8,128)} copy(f32[27,128,128]{2,1,0:T(8,128)S(1)} %bitcast.17) | data formatting | bytes 3538944 | tf_op jit(solution)/shard_map/mul | solution.py:361
  74.1 0.0 copy-done
  74.1 0.1 convert_multiply_fusion
  74.3 0.0 copy-start.1
  74.3 1.9 %copy.10 = f32[27,128,128]{1,2,0:T(8,128)} copy(f32[27,128,128]{2,1,0:T(8,128)S(1)} %bitcast.18) | data formatting | bytes 3538944 | tf_op jit(solution)/shard_map/mul | solution.py:361
  76.2 0.0 copy-done.1
  76.2 0.8 %copy.13 = bf16[2,4,16,16,128]{4,3,2,1,0:T(8,128)(2,1)} copy(bf16[2,4,16,16,128]{4,3,2,1,0:T(8,128)(2,1)S(1)} %bitcast.27) | data formatting | bytes 1048576
  (2 shorter events, 0.0 us)
Async XLA Ops:
  72.2 1.9 %copy-start = (bf16[2,2,4,224,128]{4,3,2,1,0:T(8,128)(2,1)S(1)}, bf16[2,2,4,224,128]{4,3,2,1,0:T(8,128)(2,1)}, u32[]{:S(2)}) copy-start(bf16[2,2,4,224,128]{4,3,2,1,0:T(8,128)(2,1)} %get-tuple-element.8) | copy-start | bytes 2752516
  74.3 1.9 %copy-start.1 = (bf16[2,4,256,128]{3,2,1,0:T(8,128)(2,1)S(1)}, bf16[2,4,256,128]{3,2,1,0:T(8,128)(2,1)}, u32[]{:S(2)}) copy-start(bf16[2,4,256,128]{3,2,1,0:T(8,128)(2,1)} %get-tuple-element.6) | copy-start | bytes 1572868
